TPU v7x, 128 devices: a whole 4x4x4 slice. The times are simulated.
128 devices in a mesh: seq: 8 (over y_lo, x), ctx: 16 (over y_hi, z, core).
Axes of the slice: x: 4, y: 4 (y_hi: 2, y_lo: 2; y = y_hi * 2 + y_lo), z: 4, core: 2. Of those that a mesh axis runs over, the one named last changes fastest.
Arguments:
- tokens: bfloat16 [8, 3072, 1024], P('seq', 'ctx'), may hold values from -6 to 6
- cotangent: bfloat16 [8, 3072, 1024], P('seq', 'ctx'), may hold values from -6 to 6
- w_query: bfloat16 [1024, 1024], P('seq'), may hold values from -0.1875 to 0.1875
- b_query: bfloat16 [1024], P('seq'), may hold values from -3 to 3
- w_key: bfloat16 [1024, 1024], P('seq'), may hold values from -0.1875 to 0.1875
- w_value: bfloat16 [1024, 1024], P('seq'), may hold values from -0.1875 to 0.1875
- b_value: bfloat16 [1024], P('seq'), may hold values from -3 to 3
- w_output: bfloat16 [1024, 1024], P('seq'), may hold values from -2.5 to 2.5
- b_output: bfloat16 [1024], P('seq'), may hold values from -3 to 3
- first_gain: bfloat16 [1024], P('seq'), may hold values from 0.5 to 1.5
- first_shift: bfloat16 [1024], P('seq'), may hold values from -3 to 3
- w_inner: bfloat16 [1024, 4096], P('seq'), may hold values from -0.1875 to 0.1875
- b_inner: bfloat16 [4096], P('seq'), may hold values from -3 to 3
- w_outer: bfloat16 [4096, 1024], P('seq'), may hold values from -0.09375 to 0.09375
- b_outer: bfloat16 [1024], P('seq'), may hold values from -3 to 3
- second_gain: bfloat16 [1024], P('seq'), may hold values from 0.5 to 1.5
- second_shift: bfloat16 [1024], P('seq'), may hold values from -3 to 3
Outputs:
- result: bfloat16 [8, 3072, 1024], P('seq', 'ctx')
- token_grad: float32 [8, 3072, 1024], P('seq', 'ctx')
- query_weight_grad: float32 [1024, 1024], P('seq')
- query_bias_grad: float32 [1024], P('seq')
- key_weight_grad: float32 [1024, 1024], P('seq')
- value_weight_grad: float32 [1024, 1024], P('seq')
- value_bias_grad: float32 [1024], P('seq')
- output_weight_grad: float32 [1024, 1024], P('seq')
- output_bias_grad: float32 [1024], P('seq')
- first_gain_grad: float32 [1024], P('seq')
- first_shift_grad: float32 [1024], P('seq')
- inner_weight_grad: float32 [1024, 4096], P('seq')
- inner_bias_grad: float32 [4096], P('seq')
- outer_weight_grad: float32 [4096, 1024], P('seq')
- outer_bias_grad: float32 [1024], P('seq')
- second_gain_grad: float32 [1024], P('seq')
- second_shift_grad: float32 [1024], P('seq')
All inputs are finite; a program needn't handle non-finite values.
Results may differ from a plain program's by a relative error of at most 0.028.
Values may be sent and summed in bfloat16 or wider, within the bound.
A program may use at most 192 MiB of HBM per device.

v0:
```python
import functools
import math

import jax
import jax.numpy as jnp
from jax import lax
from jax.experimental import pallas as pl
from jax.experimental.pallas import tpu as pltpu
from jax.sharding import PartitionSpec as P

D = 1024
HEADS = 16
HD = 64
FF = 4096
SEQ = 8
CHIPS = 8
ROWS = 192
PAIR = 2 * ROWS
LENGTH = CHIPS * PAIR
SCALE2 = HD ** (-0.5) * math.log2(math.e)
BLOCK = 512
BF = jnp.bfloat16
F32 = jnp.float32
ANY = pl.BlockSpec(memory_space=pl.ANY)
VMEM = pl.BlockSpec(memory_space=pltpu.VMEM)


def dot(left, right, dims=((1,), (0,))):
    return lax.dot_general(left, right, (dims, ((), ())), preferred_element_type=F32)


SIZES = {"seq": 8, "chip": 8, "x": 4, "y": 2, "z": 4, "half": 2, "core": 2}


def group_size(group):
    return SIZES[group]


def group_me(group):
    seq, ctx = lax.axis_index("seq"), lax.axis_index("ctx")
    if group == "seq":
        return seq
    if group == "x":
        return lax.rem(seq, 4)
    if group == "y":
        return lax.div(seq, 4)
    if group == "core":
        return lax.rem(ctx, 2)
    if group == "half":
        return lax.div(ctx, 8)
    if group == "z":
        return lax.rem(lax.div(ctx, 2), 4)
    return lax.div(ctx, 2)


def group_device(group, index):
    seq, ctx = lax.axis_index("seq"), lax.axis_index("ctx")
    if group == "seq":
        return (index, ctx)
    if group == "x":
        return (lax.div(seq, 4) * 4 + index, ctx)
    if group == "y":
        return (index * 4 + lax.rem(seq, 4), ctx)
    if group == "core":
        return (seq, lax.div(ctx, 2) * 2 + index)
    if group == "half":
        return (seq, index * 8 + lax.rem(ctx, 8))
    if group == "z":
        return (seq, lax.div(ctx, 8) * 8 + index * 2 + lax.rem(ctx, 2))
    return (seq, index * 2 + lax.rem(ctx, 2))


def group_peer(group, step):
    return lax.rem(group_me(group) + step, group_size(group))


def enter(groups):
    barrier = pltpu.get_barrier_semaphore()
    count = 0
    for group in groups:
        for step in range(1, group_size(group)):
            pl.semaphore_signal(
                barrier,
                inc=1,
                device_id=group_device(group, group_peer(group, step)),
                device_id_type=pl.DeviceIdType.MESH,
            )
            count += 1
    pl.semaphore_wait(barrier, count)


def remote(source, target, send, recv, group, peer):
    return pltpu.make_async_remote_copy(
        src_ref=source,
        dst_ref=target,
        send_sem=send,
        recv_sem=recv,
        device_id=group_device(group, peer),
        device_id_type=pl.DeviceIdType.MESH,
    )


def dma(*shape):
    return pltpu.SemaphoreType.DMA(shape)


class Exchange:
    def __init__(self, kind, group, source, target, refs, rows=None):
        self.kind, self.group = kind, group
        self.source, self.target, self.rows = source, target, rows
        self.send, self.recv = refs[:2]
        if rows is None:
            self.own, self.own_held = refs[2:]

    @staticmethod
    def scratch(kind, group, value, rows=None):
        count = group_size(group) - 1
        if rows is not None:
            return [dma(count), dma(count)]
        piece = value.shape if kind == "ag" else value.shape[1:]
        return [dma(count), dma(count), dma(2), pltpu.VMEM(piece, value.dtype)]

    def copies(self):
        me = group_me(self.group)
        made = []
        for step in range(1, group_size(self.group)):
            peer = group_peer(self.group, step)
            piece = self.source if self.kind == "ag" else self.source.at[peer]
            target = self.target.at[me]
            if self.rows is not None:
                piece, target = piece.at[pl.ds(*self.rows)], target.at[pl.ds(*self.rows)]
            made.append(
                remote(piece, target, self.send.at[step - 1], self.recv.at[step - 1], self.group, peer)
            )
        return made

    def own_copies(self):
        me = group_me(self.group)
        piece = self.source if self.kind == "ag" else self.source.at[me]
        return (
            pltpu.make_async_copy(piece, self.own_held, self.own.at[0]),
            pltpu.make_async_copy(self.own_held, self.target.at[me], self.own.at[1]),
        )

    def start(self):
        for copy in self.copies():
            copy.start()
        if self.rows is None:
            self.own_copies()[0].start()

    def wait(self):
        if self.rows is None:
            own_in, own_out = self.own_copies()
            own_in.wait()
            own_out.start()
            own_out.wait()
        for copy in self.copies():
            copy.wait()


class Own:
    def __init__(self, source, target, refs):
        self.source, self.target = source, target.at[group_me("seq")]
        self.sems, self.held = refs

    @staticmethod
    def scratch(value):
        return [dma(2), pltpu.VMEM(value.shape, value.dtype)]

    def start(self):
        pltpu.make_async_copy(self.source, self.held, self.sems.at[0]).start()

    def wait(self):
        pltpu.make_async_copy(self.source, self.held, self.sems.at[0]).wait()
        copy = pltpu.make_async_copy(self.held, self.target, self.sems.at[1])
        copy.start()
        copy.wait()


class RelayGather:
    def __init__(self, source, target, span, order, refs):
        self.source, self.target, self.span, self.order = source, target, span, order
        self.send, self.recv = refs
        x, y = group_me("x"), group_me("y")
        back = [lax.rem(x + 4 - step, 4) for step in range(1, 4)]
        if order == "yx":
            self.owners = [(1 - y) * 4 + x] + [y * 4 + at for at in back] + [(1 - y) * 4 + at for at in back]
        else:
            self.owners = [y * 4 + at for at in back] + [(1 - y) * 4 + x] + [(1 - y) * 4 + at for at in back]

    @staticmethod
    def scratch():
        return [dma(7), dma(7)]

    def slot(self, at):
        x, y = group_me("x"), group_me("y")
        piece = self.source.at[self.span]
        place = self.target.at[y * 4 + x, self.span]
        if self.order == "yx":
            group, step = ("y", 1) if at == 0 else ("x", (at - 1) % 3 + 1)
            if at >= 4:
                piece = place = self.target.at[self.owners[0], self.span]
        else:
            group, step = ("x", at + 1) if at < 3 else ("y", 1)
            if at >= 4:
                piece = place = self.target.at[self.owners[at - 4], self.span]
        return remote(piece, place, self.send.at[at], self.recv.at[at], group, group_peer(group, step))

    def start(self):
        for at in range(4):
            self.slot(at).start()

    def forward(self):
        if self.order == "yx":
            self.slot(0).wait_recv()
            for at in range(4, 7):
                self.slot(at).start()
        else:
            for at in range(3):
                self.slot(at).wait_recv()
                self.slot(at + 4).start()

    def waited(self):
        return (0,) if self.order == "yx" else (0, 1, 2)

    def wait_recv(self):
        for at in range(7):
            if at not in self.waited():
                self.slot(at).wait_recv()

    def wait_send(self):
        for at in range(7):
            self.slot(at).wait_send()

    def wait(self):
        self.wait_recv()
        self.wait_send()


class SplitGather:
    def __init__(self, source, target, refs):
        rows = source.shape[0] // 4
        self.span = pl.ds(pl.multiple_of(group_me("z") * rows, 16), rows)
        self.target = target
        self.relay = RelayGather(source, target, self.span, "yx", refs[:2])
        self.send, self.recv = refs[2:]

    @staticmethod
    def scratch():
        return RelayGather.scratch() + [dma(21), dma(21)]

    def second(self, slot, hop):
        at = slot * 3 + hop - 1
        piece = self.target.at[self.relay.owners[slot], self.span]
        return remote(piece, piece, self.send.at[at], self.recv.at[at], "z", group_peer("z", hop))

    def start(self):
        self.relay.start()

    def forward_x(self):
        self.relay.forward()
        for hop in range(1, 4):
            self.second(0, hop).start()

    def forward_z(self):
        for slot in range(1, 7):
            self.relay.slot(slot).wait_recv()
            for hop in range(1, 4):
                self.second(slot, hop).start()

    def wait(self):
        self.relay.wait_send()
        for slot in range(7):
            for hop in range(1, 4):
                self.second(slot, hop).wait()


class RelayReduce:
    def __init__(self, source, rows, order, refs):
        self.source, self.span, self.order = source, pl.ds(*rows), order
        self.group, self.group_two = order
        self.size, self.size_two = group_size(order[0]), group_size(order[1])
        self.send, self.recv, self.local, self.got, self.total, self.send_two, self.recv_two, self.got_two = refs

    @staticmethod
    def scratch(value, rows, order):
        piece, kind = (rows[1], value.shape[2]), value.dtype
        one, two = group_size(order[0]), group_size(order[1])
        pieces = (one - 1) * two
        return [
            dma(pieces),
            dma(pieces),
            dma(two),
            pltpu.VMEM((pieces,) + piece, kind),
            pltpu.VMEM((two,) + piece, kind),
            dma(two - 1),
            dma(two - 1),
            pltpu.VMEM((two - 1,) + piece, kind),
        ]

    def piece(self, one, two):
        return self.source.at[one * 4 + two if self.order == "yx" else two * 4 + one, self.span]

    def first(self):
        made = []
        for step in range(1, self.size):
            peer = group_peer(self.group, step)
            for two in range(self.size_two):
                at = (step - 1) * self.size_two + two
                made.append(
                    remote(
                        self.piece(peer, two), self.got.at[at], self.send.at[at], self.recv.at[at], self.group, peer
                    )
                )
        return made

    def own(self):
        return [
            pltpu.make_async_copy(
                self.piece(group_me(self.group), two), self.total.at[two], self.local.at[two]
            )
            for two in range(self.size_two)
        ]

    def second(self):
        made = []
        for step in range(1, self.size_two):
            peer = group_peer(self.group_two, step)
            made.append(
                remote(
                    self.total.at[peer],
                    self.got_two.at[step - 1],
                    self.send_two.at[step - 1],
                    self.recv_two.at[step - 1],
                    self.group_two,
                    peer,
                )
            )
        return made

    def start(self):
        for copy in self.first() + self.own():
            copy.start()

    def forward(self):
        for copy in self.own() + self.first():
            copy.wait()
        for two in range(self.size_two):
            value = self.total[two].astype(F32)
            for step in range(self.size - 1):
                value += self.got[step * self.size_two + two].astype(F32)
            self.total[two] = value.astype(self.total.dtype)
        for copy in self.second():
            copy.start()

    def sum(self):
        for copy in self.second():
            copy.wait()
        value = self.total[group_me(self.group_two)].astype(F32)
        for step in range(self.size_two - 1):
            value += self.got_two[step].astype(F32)
        return value


class SplitReduce:
    def __init__(self, source, refs):
        self.source, self.quarter = source, source.shape[1] // 4
        self.send, self.recv, self.local, self.got, self.total = refs[:5]
        self.relay = RelayReduce(self.total, (0, self.quarter), "xy", refs[5:])

    @staticmethod
    def scratch(value):
        quarter, columns = value.shape[1] // 4, value.shape[2]
        return [dma(3), dma(3), dma()] + [
            pltpu.VMEM((3, 8, quarter, columns), BF),
            pltpu.VMEM((8, quarter, columns), BF),
        ] + RelayReduce.scratch(value, (0, quarter), "xy")

    def part(self, index):
        return self.source.at[:, pl.ds(pl.multiple_of(index * self.quarter, 16), self.quarter)]

    def first(self, hop):
        peer = group_peer("z", hop)
        return remote(
            self.part(peer), self.got.at[hop - 1], self.send.at[hop - 1], self.recv.at[hop - 1], "z", peer
        )

    def own_copy(self):
        return pltpu.make_async_copy(self.part(group_me("z")), self.total, self.local)

    def start(self):
        for hop in range(1, 4):
            self.first(hop).start()
        self.own_copy().start()

    def forward_z(self):
        self.own_copy().wait()
        for hop in range(1, 4):
            self.first(hop).wait()

        def add(at, carry):
            value = self.total[at].astype(F32)
            for hop in range(3):
                value += self.got[hop, at].astype(F32)
            self.total[at] = value.astype(BF)
            return carry

        lax.fori_loop(0, 8, add, 0)
        self.relay.start()

    def forward(self):
        self.relay.forward()

    def sum(self):
        return self.relay.sum()


class Refs:
    def __init__(self, refs):
        self.refs, self.at = refs, 0

    def take(self, count):
        self.at += count
        return self.refs[self.at - count : self.at]

    def left(self):
        return self.refs[self.at :]


def target_shape(kind, group, value):
    shape = value.shape if kind == "a2a" else (group_size(group),) + value.shape
    return jax.ShapeDtypeStruct(shape, value.dtype)


def params(identifier, mebibytes):
    return pltpu.CompilerParams(
        collective_id=identifier,
        has_side_effects=True,
        vmem_limit_bytes=mebibytes * 1024 * 1024,
    )


def forward(identifier, rows, w_query, w_key, w_value, small_part, w_output, w_inner, w_outer):
    columns = SEQ * 3 * HD
    qkv_part = jax.ShapeDtypeStruct((128, columns), BF)
    heads_shape = jax.ShapeDtypeStruct((CHIPS, 3 * HD, PAIR), BF)
    low_shape = jax.ShapeDtypeStruct((CHIPS, HD, PAIR), BF)
    output_part = jax.ShapeDtypeStruct((HD, D), BF)
    inner_part = jax.ShapeDtypeStruct((128, FF // 2), BF)
    outer_part = jax.ShapeDtypeStruct((256, D), BF)

    def kernel(*refs):
        refs = Refs(refs)
        rows_ref, query_ref, key_ref, value_ref, small_ref, output_ref, inner_ref, outer_ref = refs.take(8)
        turned_out, qkv_out, small_out, bias_out, output_out, inner_out, outer_out = refs.take(7)
        qkv_got, summed_ref, back_ref, stat_ref = refs.take(4)
        qkv_ref, inner_held, rows_out, small_got, heads, query_t, keys, value_t, low = refs.take(9)
        core = group_me("core")

        def mine(value, axis):
            half = value.shape[axis] // 2
            low_half = lax.slice_in_dim(value, 0, half, axis=axis)
            return jnp.where(core == 0, low_half, lax.slice_in_dim(value, half, 2 * half, axis=axis))

        output_ref = output_ref.at[pl.ds(pl.multiple_of(core * HD, HD), HD)]
        outer_ref = outer_ref.at[pl.ds(pl.multiple_of(core * 256, 256), 256)]
        split = SplitGather(qkv_ref.at[pl.ds(0, 64)], qkv_out, refs.take(4))
        one_way = RelayGather(qkv_ref, qkv_out, pl.ds(64, 32), "yx", refs.take(2))
        other_way = RelayGather(qkv_ref, qkv_out, pl.ds(96, 32), "xy", refs.take(2))
        qkv_own = Own(qkv_ref, qkv_out, refs.take(2))
        small = Exchange("ag", "seq", small_ref, small_got, refs.take(4))
        pair = Exchange("ag", "core", rows_ref, rows_out, refs.take(4))
        first = Exchange("a2a", "chip", heads, qkv_got, refs.take(4))
        last = Exchange("a2a", "chip", low, back_ref, refs.take(4))
        inner = SplitGather(inner_held, inner_out, refs.take(4))
        output = RelayGather(output_ref, output_out, pl.ds(0, HD), "yx", refs.take(2))
        outer_one = RelayGather(outer_ref, outer_out, pl.ds(0, 128), "yx", refs.take(2))
        outer_two = RelayGather(outer_ref, outer_out, pl.ds(128, 128), "xy", refs.take(2))
        owns = [
            Own(source, target, refs.take(2))
            for source, target in (
                (output_ref, output_out),
                (inner_held, inner_out),
                (outer_ref, outer_out),
            )
        ]
        for owner in range(0, SEQ, 2):
            parts = []
            for head in (owner, owner + 1):
                for ref in (query_ref, key_ref, value_ref):
                    parts.append(mine(ref[:, head * 128 : (head + 1) * 128].astype(F32), 1))
            qkv_ref[:, owner * 192 : (owner + 2) * 192] = jnp.concatenate(parts, axis=1).astype(BF)
        enter(["seq", "chip", "core"])
        for one in (split, one_way, other_way, qkv_own, small, pair):
            one.start()
        for owner in range(SEQ):
            here = pl.ds(pl.multiple_of(owner * 512 + core * 256, 256), 256)
            inner_held[:, owner * 256 : (owner + 1) * 256] = inner_ref[:, here]
        for own in owns:
            own.start()
        split.forward_x()
        one_way.forward()
        split.forward_z()
        inner.start()
        outer_two.start()
        other_way.forward()
        for one in (pair, small, qkv_own, one_way, other_way, split):
            one.wait()
        inner.forward_x()
        weight = qkv_out[...].reshape(D, columns)
        turned = dot(rows_out[...].reshape(PAIR, D), weight).T
        for chip in range(CHIPS):
            shift = mine(small_got[chip].astype(F32).T, 0)
            part = turned[chip * 3 * HD : (chip + 1) * 3 * HD]
            heads[chip, 0:HD, :] = (part[:HD] + shift[:, 0:1]).astype(BF)
            heads[chip, HD : 2 * HD, :] = part[HD : 2 * HD].astype(BF)
            heads[chip, 2 * HD :, :] = (part[2 * HD :] + shift[:, 1:2]).astype(BF)
        first.start()
        output.start()
        outer_one.start()
        inner.forward_z()
        output.forward()
        turned_out[...] = rows_out[...].reshape(PAIR, D).astype(F32).T.astype(BF)
        for owner in range(SEQ):
            at = slice(owner * 128, (owner + 1) * 128)
            values = small_got[owner].astype(F32)
            small_out[:, at] = values[2:10]
            for row in range(2):
                at = slice(owner * 256 + row * 128, owner * 256 + (row + 1) * 128)
                bias_out[:, at] = jnp.where(core == 0, values[8 + row : 9 + row], values[10 + row : 11 + row])
        first.wait()
        for chip in range(CHIPS):
            at = pl.ds(chip * PAIR, PAIR)
            query_t[:, at] = qkv_got[chip, 0:HD, :]
            keys[at, :] = qkv_got[chip, HD : 2 * HD, :].astype(F32).T.astype(BF)
            value_t[:, at] = qkv_got[chip, 2 * HD : 3 * HD, :]
        outer_one.forward()

        def one_block(block, carry):
            at = pl.ds(pl.multiple_of(block * BLOCK, BLOCK), BLOCK)
            query = query_t[:, at]
            top = jnp.full((1, BLOCK), -1e30, F32)
            total = jnp.zeros((1, BLOCK), F32)
            summed = jnp.zeros((HD, BLOCK), F32)
            for part in range(LENGTH // BLOCK):
                here = slice(part * BLOCK, (part + 1) * BLOCK)
                scores = dot(keys[here, :], query) * SCALE2
                new_top = jnp.maximum(top, jnp.max(scores, axis=0, keepdims=True))
                factor = jnp.exp2(top - new_top)
                weights = jnp.exp2(scores - new_top)
                total = total * factor + jnp.sum(weights, axis=0, keepdims=True)
                summed = summed * factor + dot(value_t[:, here], weights.astype(BF))
                top = new_top
            summed_ref[:, at] = summed / total
            stat_ref[:, at] = top + jnp.log2(total)
            return carry

        lax.fori_loop(0, 2, one_block, 0)
        outer_two.forward()
        lax.fori_loop(2, LENGTH // BLOCK, one_block, 0)
        for chip in range(CHIPS):
            low[chip] = summed_ref[:, chip * PAIR : (chip + 1) * PAIR].astype(BF)
        last.start()
        for one in [last, output, inner, outer_one, outer_two] + owns:
            one.wait()

    return pl.pallas_call(
        kernel,
        out_shape=[
            jax.ShapeDtypeStruct((D, PAIR), BF),
            target_shape("ag", "seq", qkv_part),
            jax.ShapeDtypeStruct((8, D), F32),
            jax.ShapeDtypeStruct((1, FF // 2), F32),
            target_shape("ag", "seq", output_part),
            target_shape("ag", "seq", inner_part),
            target_shape("ag", "seq", outer_part),
            heads_shape,
            jax.ShapeDtypeStruct((HD, LENGTH), F32),
            low_shape,
            jax.ShapeDtypeStruct((1, LENGTH), F32),
        ],
        in_specs=[ANY] + [VMEM] * 3 + [ANY] * 2 + [VMEM, ANY],
        out_specs=[VMEM] * 4 + [ANY] * 3 + [VMEM] * 4,
        scratch_shapes=[
            pltpu.VMEM(qkv_part.shape, BF),
            pltpu.VMEM(inner_part.shape, BF),
            pltpu.VMEM((2, ROWS, D), BF),
            pltpu.VMEM((SEQ, 16, 128), BF),
            pltpu.VMEM(heads_shape.shape, BF),
            pltpu.VMEM((HD, LENGTH), BF),
            pltpu.VMEM((LENGTH, HD), BF),
            pltpu.VMEM((HD, LENGTH), BF),
            pltpu.VMEM(low_shape.shape, BF),
        ]
        + SplitGather.scratch()
        + RelayGather.scratch()
        + RelayGather.scratch()
        + Own.scratch(qkv_part)
        + Exchange.scratch("ag", "seq", small_part)
        + Exchange.scratch("ag", "core", rows)
        + Exchange.scratch("a2a", "chip", heads_shape)
        + Exchange.scratch("a2a", "chip", low_shape)
        + SplitGather.scratch()
        + RelayGather.scratch()
        + RelayGather.scratch()
        + RelayGather.scratch()
        + Own.scratch(output_part)
        + Own.scratch(inner_part)
        + Own.scratch(outer_part),
        compiler_params=params(identifier, 48),
        name="forward",
    )(rows, w_query, w_key, w_value, small_part, w_output, w_inner, w_outer)


class Scatter:
    def __init__(self, group, source, refs):
        self.group, self.source = group, source
        send, recv, self.got = refs
        self.copies = [
            remote(
                source.at[group_peer(group, step)],
                self.got.at[step - 1],
                send.at[step - 1],
                recv.at[step - 1],
                group,
                group_peer(group, step),
            )
            for step in range(1, group_size(group))
        ]

    @staticmethod
    def scratch(group, piece, kind):
        count = group_size(group) - 1
        return [dma(count), dma(count), pltpu.VMEM((count,) + piece, kind)]

    def start(self):
        for copy in self.copies:
            copy.start()

    def sum(self):
        for copy in self.copies:
            copy.wait()
        own = self.source[group_me(self.group)].astype(F32)
        return sum((self.got[at].astype(F32) for at in range(group_size(self.group) - 1)), own)


class Swap:
    def __init__(self, group, source, refs):
        send, recv, self.got = refs
        self.source = source
        self.copy = remote(source, self.got, send, recv, group, group_peer(group, 1))

    @staticmethod
    def scratch(piece, kind):
        return [dma(), dma(), pltpu.VMEM(piece, kind)]

    def start(self):
        self.copy.start()

    def sum(self):
        self.copy.wait()
        return self.source[...].astype(F32) + self.got[...].astype(F32)


class Spread:
    def __init__(self, group, held, refs):
        send, recv, send_core, recv_core = refs
        self.group, self.held = group, held
        mine = held.at[group_me("core")]
        self.mine = mine
        piece = mine.at[group_me(group)]
        self.copies = [
            remote(piece, piece, send.at[step - 1], recv.at[step - 1], group, group_peer(group, step))
            for step in range(1, group_size(group))
        ]
        self.last = remote(mine, mine, send_core, recv_core, "core", group_peer("core", 1))

    @staticmethod
    def scratch(group):
        count = group_size(group) - 1
        return [dma(count), dma(count), dma(), dma()]

    def start(self, value):
        self.mine[group_me(self.group)] = value.astype(self.held.dtype)
        for copy in self.copies:
            copy.start()

    def forward(self):
        for copy in self.copies:
            copy.wait()
        self.last.start()

    def wait(self):
        self.last.wait()


def backward(
    identifier,
    qkv_got,
    summed,
    stat,
    grad,
    rows_t,
    qkv_weight,
    residual,
    row_sums,
    bias_sums,
    output_grad,
    inner_grad,
    outer_grad,
):
    columns = SEQ * 3 * HD
    half = 64
    chip_piece = (16, columns)
    vector = (8, 128)
    grads_shape = jax.ShapeDtypeStruct((SEQ, 128, columns), BF)
    inner_half_shape = jax.ShapeDtypeStruct((SEQ, 64, FF // 2), BF)

    def kernel(*refs):
        refs = Refs(refs)
        qkv_ref, summed_ref, stat_ref, grad_ref, rows_ref, weight_ref = refs.take(6)
        residual_ref, row_sums_ref, bias_sums_ref = refs.take(3)
        output_ref, inner_ref, outer_ref = refs.take(3)
        token_out, qkv_out, output_out, inner_out, outer_out, vector_out, bias_out = refs.take(7)
        grad_got, heads_got, query_t, queries, key_t, keys, values, up_t, ups, delta_ref = refs.take(10)
        grad_query, grad_key, grad_value, low = refs.take(4)
        vectors_ref, grads, bias, partial, token_got, token_send, token_recv = refs.take(7)
        output_sum, outer_sum, output_mine, inner_mine, outer_mine, qkv_sum = refs.take(6)
        first = Exchange("a2a", "chip", grad_ref, grad_got, refs.take(4))
        last = Exchange("a2a", "chip", low, heads_got, refs.take(4))
        inner_one = SplitReduce(inner_ref.at[:, pl.ds(0, 64)], refs.take(13))
        inner_two = SplitReduce(inner_ref.at[:, pl.ds(64, 64)], refs.take(13))
        output = RelayReduce(output_ref, (0, HD), "xy", refs.take(8))
        outer_one = RelayReduce(outer_ref, (0, 128), "xy", refs.take(8))
        outer_two = RelayReduce(outer_ref, (128, 128), "yx", refs.take(8))
        qkv_one = RelayReduce(grads, (0, half), "xy", refs.take(8))
        qkv_two = RelayReduce(grads, (half, half), "yx", refs.take(8))
        vector_seq = Scatter("seq", vectors_ref, refs.take(3))
        bias_seq = Scatter("seq", bias, refs.take(3))
        output_z = Scatter("z", output_sum, refs.take(3))
        outer_z = Scatter("z", outer_sum, refs.take(3))
        output_half = Swap("half", output_mine, refs.take(3))
        outer_half = Swap("half", outer_mine, refs.take(3))
        inner_half = Swap("half", inner_mine, refs.take(3))
        qkv_chip = Scatter("chip", qkv_sum, refs.take(3))
        output_all = Spread("z", output_out, refs.take(4))
        outer_all = Spread("z", outer_out, refs.take(4))
        inner_all = Spread("z", inner_out, refs.take(4))
        qkv_all = Spread("chip", qkv_out, refs.take(4))
        vector_all = Spread("chip", vector_out, refs.take(4))
        bias_all = Spread("chip", bias_out, refs.take(4))
        other = group_peer("core", 1)
        token = remote(partial.at[other], token_got, token_send, token_recv, "core", other)

        for owner in range(SEQ):
            vectors_ref[owner, 0:6, :] = row_sums_ref[0:6, owner * 128 : (owner + 1) * 128]
            for row in range(2):
                at = slice(owner * 256 + row * 128, owner * 256 + (row + 1) * 128)
                vectors_ref[owner, 6 + row : 7 + row, :] = bias_sums_ref[:, at]
        enter(["seq", "chip", "core"])
        for one in (first, inner_one, outer_two, output, outer_one, vector_seq):
            one.start()
        for chip in range(CHIPS):
            at = pl.ds(chip * PAIR, PAIR)
            query_t[:, at] = qkv_ref[chip, 0:HD, :]
            queries[at, :] = qkv_ref[chip, 0:HD, :].astype(F32).T.astype(BF)
            key_t[:, at] = qkv_ref[chip, HD : 2 * HD, :]
            keys[at, :] = qkv_ref[chip, HD : 2 * HD, :].astype(F32).T.astype(BF)
            values[at, :] = qkv_ref[chip, 2 * HD : 3 * HD, :].astype(F32).T.astype(BF)
        grad_key[...] = jnp.zeros_like(grad_key)
        grad_value[...] = jnp.zeros_like(grad_value)
        first.wait()
        for chip in range(CHIPS):
            at = pl.ds(chip * PAIR, PAIR)
            up = grad_got[chip].astype(F32)
            up_t[:, at] = grad_got[chip]
            ups[at, :] = up.T.astype(BF)
            delta_ref[:, at] = jnp.sum(up * summed_ref[:, at], axis=0, keepdims=True)

        def one_block(block, carry):
            at = pl.ds(pl.multiple_of(block * BLOCK, BLOCK), BLOCK)
            query, up = query_t[:, at], up_t[:, at]
            query_rows, up_rows = queries[at, :], ups[at, :]
            stat, delta = stat_ref[:, at], delta_ref[:, at]
            gathered = jnp.zeros((HD, BLOCK), F32)
            for part in range(LENGTH // BLOCK):
                here = slice(part * BLOCK, (part + 1) * BLOCK)
                scores = dot(keys[here, :], query) * SCALE2
                probs = jnp.exp2(scores - stat)
                grad_value[here, :] += dot(probs.astype(BF), up_rows)
                slope = dot(values[here, :], up) - delta
                grad_scores = (probs * slope).astype(BF)
                grad_key[here, :] += dot(grad_scores, query_rows)
                gathered += dot(key_t[:, here], grad_scores)
            grad_query[:, at] = gathered
            return carry

        lax.fori_loop(0, LENGTH // BLOCK, one_block, 0)
        scale = HD ** (-0.5)
        for chip in range(CHIPS):
            at = slice(chip * PAIR, (chip + 1) * PAIR)
            low[chip, 0:HD, :] = (grad_query[:, at] * scale).astype(BF)
            low[chip, HD : 2 * HD, :] = (grad_key[at, :] * scale).T.astype(BF)
            low[chip, 2 * HD : 3 * HD, :] = grad_value[at, :].T.astype(BF)
        last.start()
        output.forward()
        outer_two.forward()
        outer_one.forward()
        vector_all.start(vector_seq.sum())
        last.wait()

        heads = heads_got[...].reshape(columns, PAIR)

        def weight_rows(owner, carry):
            at = pl.ds(pl.multiple_of(owner * 128, 128), 128)
            grads[owner] = dot(rows_ref[at, :], heads, ((1,), (1,))).astype(BF)
            bias[owner] = dot(jnp.ones((8, PAIR), BF), heads_got[owner], ((1,), (1,)))
            return carry

        lax.fori_loop(0, SEQ, weight_rows, 0)
        qkv_two.start()
        qkv_one.start()
        bias_seq.start()
        inner_one.forward_z()
        inner_two.start()
        output_sum[...] = output.sum().astype(BF).reshape(output_sum.shape)
        output_z.start()
        outer_sum[2:] = outer_two.sum().astype(BF).reshape(2, 64, D)
        outer_sum[:2] = outer_one.sum().astype(BF).reshape(2, 64, D)
        outer_z.start()
        turned = dot(weight_ref[...].reshape(D, columns), heads).T
        partial[0] = turned[:ROWS]
        partial[1] = turned[ROWS:]
        token.start()
        qkv_two.forward()
        qkv_one.forward()
        inner_one.forward()
        output_mine[...] = output_z.sum().astype(BF)
        output_half.start()
        outer_mine[...] = outer_z.sum().astype(BF)
        outer_half.start()
        bias_all.start(bias_seq.sum())
        upper = qkv_one.sum().reshape(CHIPS, 8, columns)
        lower = qkv_two.sum().reshape(CHIPS, 8, columns)
        qkv_sum[...] = jnp.concatenate([upper, lower], axis=1).astype(BF)
        qkv_chip.start()
        inner_two.forward_z()
        output_all.start(output_half.sum())
        outer_all.start(outer_half.sum())
        inner_mine[:16] = inner_one.sum().astype(BF)
        token.wait()
        token_out[...] = residual_ref[...] + partial[group_me("core")] + token_got[...]
        qkv_all.start(qkv_chip.sum())
        inner_two.forward()
        vector_all.forward()
        bias_all.forward()
        inner_mine[16:] = inner_two.sum().astype(BF)
        inner_half.start()
        output_all.forward()
        outer_all.forward()
        qkv_all.forward()
        inner_all.start(inner_half.sum())
        inner_all.forward()
        for one in (vector_all, bias_all, output_all, outer_all, qkv_all, inner_all):
            one.wait()

    return pl.pallas_call(
        kernel,
        out_shape=[
            jax.ShapeDtypeStruct((ROWS, D), F32),
            jax.ShapeDtypeStruct((2, CHIPS) + chip_piece, BF),
            jax.ShapeDtypeStruct((2, 4, 16, D), BF),
            jax.ShapeDtypeStruct((2, 4, 32, FF // 2), BF),
            jax.ShapeDtypeStruct((2, 4, 64, D), BF),
            jax.ShapeDtypeStruct((2, CHIPS) + vector, F32),
            jax.ShapeDtypeStruct((2, CHIPS, 8, 3 * HD), F32),
        ],
        in_specs=[VMEM] * 9 + [ANY] * 3,
        out_specs=[VMEM] * 7,
        scratch_shapes=[
            pltpu.VMEM(grad.shape, BF),
            pltpu.VMEM(qkv_got.shape, BF),
            pltpu.VMEM((HD, LENGTH), BF),
            pltpu.VMEM((LENGTH, HD), BF),
            pltpu.VMEM((HD, LENGTH), BF),
            pltpu.VMEM((LENGTH, HD), BF),
            pltpu.VMEM((LENGTH, HD), BF),
            pltpu.VMEM((HD, LENGTH), BF),
            pltpu.VMEM((LENGTH, HD), BF),
            pltpu.VMEM((1, LENGTH), F32),
            pltpu.VMEM((HD, LENGTH), F32),
            pltpu.VMEM((LENGTH, HD), F32),
            pltpu.VMEM((LENGTH, HD), F32),
            pltpu.VMEM((CHIPS, 3 * HD, PAIR), BF),
            pltpu.VMEM((SEQ,) + vector, F32),
            pltpu.VMEM((SEQ, 128, columns), BF),
            pltpu.VMEM((SEQ, 8, 3 * HD), F32),
            pltpu.VMEM((2, ROWS, D), F32),
            pltpu.VMEM((ROWS, D), F32),
            dma(),
            dma(),
            pltpu.VMEM((4, 16, D), BF),
            pltpu.VMEM((4, 64, D), BF),
            pltpu.VMEM((16, D), BF),
            pltpu.VMEM((32, FF // 2), BF),
            pltpu.VMEM((64, D), BF),
            pltpu.VMEM((CHIPS,) + chip_piece, BF),
        ]
        + Exchange.scratch("a2a", "chip", grad)
        + Exchange.scratch("a2a", "chip", qkv_got)
        + SplitReduce.scratch(inner_half_shape)
        + SplitReduce.scratch(inner_half_shape)
        + RelayReduce.scratch(output_grad, (0, HD), "xy")
        + RelayReduce.scratch(outer_grad, (0, 128), "xy")
        + RelayReduce.scratch(outer_grad, (128, 128), "yx")
        + RelayReduce.scratch(grads_shape, (0, half), "xy")
        + RelayReduce.scratch(grads_shape, (half, half), "yx")
        + Scatter.scratch("seq", vector, F32)
        + Scatter.scratch("seq", (8, 3 * HD), F32)
        + Scatter.scratch("z", (16, D), BF)
        + Scatter.scratch("z", (64, D), BF)
        + Swap.scratch((16, D), BF)
        + Swap.scratch((64, D), BF)
        + Swap.scratch((32, FF // 2), BF)
        + Scatter.scratch("chip", chip_piece, BF)
        + Spread.scratch("z")
        + Spread.scratch("z")
        + Spread.scratch("z")
        + Spread.scratch("chip")
        + Spread.scratch("chip")
        + Spread.scratch("chip"),
        compiler_params=params(identifier, 56),
        name="backward",
    )(
        qkv_got,
        summed,
        stat,
        grad,
        rows_t,
        qkv_weight,
        residual,
        row_sums,
        bias_sums,
        output_grad,
        inner_grad,
        outer_grad,
    )


def unpack(qkv, output, inner, outer, vectors, biases):
    def kernel(*refs):
        refs = Refs(refs)
        qkv_ref, output_ref, inner_ref, outer_ref, vectors_ref, biases_ref = refs.take(6)
        query, key, value, output_out, inner_out, outer_out = refs.take(6)
        query_bias, value_bias, inner_bias = refs.take(3)
        vector = [jnp.sum(vectors_ref[core], axis=0) for core in range(2)]
        bias = [jnp.sum(biases_ref[core], axis=0)[0:1] for core in range(2)]
        for row, out in enumerate(refs.left()):
            out[...] = vector[0][row : row + 1] + vector[1][row : row + 1]
        query_bias[...] = jnp.concatenate([part[:, :HD] for part in bias], axis=1)
        value_bias[...] = jnp.concatenate([part[:, 2 * HD :] for part in bias], axis=1)
        for core in range(2):
            for row in range(2):
                start = core * 256 + row * 128
                inner_bias[:, start : start + 128] = vector[core][6 + row : 7 + row]

        def place(pair, rows):
            for kind, out in enumerate((query, key, value)):
                for head in range(SEQ):
                    at = head * 3 * HD + kind * HD
                    out[rows, head * 128 : (head + 1) * 128] = jnp.concatenate(
                        [part[:, at : at + HD] for part in pair], axis=1
                    )

        for chip in range(CHIPS):
            pair = [qkv_ref[core, chip].astype(F32) for core in range(2)]
            place([part[:8] for part in pair], slice(chip * 8, (chip + 1) * 8))
            place([part[8:] for part in pair], slice(64 + chip * 8, 64 + (chip + 1) * 8))
        for core in range(2):
            for quarter in range(4):
                start = core * HD + quarter * 16
                output_out[start : start + 16] = output_ref[core, quarter].astype(F32)
                start = core * 256 + quarter * 64
                outer_out[start : start + 64] = outer_ref[core, quarter].astype(F32)
                for half in range(2):
                    rows = slice(half * 64 + quarter * 16, half * 64 + (quarter + 1) * 16)
                    for owner in range(SEQ):
                        start = owner * 512 + core * 256
                        inner_out[rows, start : start + 256] = inner_ref[
                            core, quarter, half * 16 : (half + 1) * 16, owner * 256 : (owner + 1) * 256
                        ].astype(F32)

    shapes = [(128, D)] * 4 + [(128, FF), (512, D), (1, 128), (1, 128), (1, 512)] + [(1, 128)] * 6
    return pl.pallas_call(
        kernel,
        out_shape=[jax.ShapeDtypeStruct(shape, F32) for shape in shapes],
        in_specs=[VMEM] * 6,
        out_specs=[VMEM] * 15,
        compiler_params=pltpu.CompilerParams(vmem_limit_bytes=32 * 1024 * 1024),
        name="unpack",
    )(qkv, output, inner, outer, vectors, biases)


def normalize(hidden):
    centered = hidden - jnp.mean(hidden, axis=-1, keepdims=True)
    inverse = lax.rsqrt(jnp.mean(centered * centered, axis=-1, keepdims=True) + 1e-05)
    return centered * inverse, inverse


def normalize_back(upstream, normed, inverse, gain):
    scaled = upstream * gain
    return inverse * (
        scaled
        - jnp.mean(scaled, axis=-1, keepdims=True)
        - normed * jnp.mean(scaled * normed, axis=-1, keepdims=True)
    )


def sum_rows(value):
    return jnp.sum(value, axis=0, keepdims=True)


def feed_forward(identifier, rows, cotangent, attended, output_weight, inner_weight, outer_weight, small, inner_bias):
    units, tile = FF // 2, 512

    def kernel(*refs):
        refs = Refs(refs)
        rows_ref, upstream_ref, attended_ref, small_ref, bias_ref = refs.take(5)
        output_hbm, inner_hbm, outer_hbm = refs.take(3)
        result_ref, residual_ref, turned_ref, sums_ref, bias_sum_ref = refs.take(5)
        grad_output_hbm, grad_inner_hbm, grad_outer_hbm = refs.take(3)
        output_w, inner_w, outer_w, load_sems = refs.take(4)
        grad_output, grad_inner, grad_outer, store_sems = refs.take(4)
        partial, got, pairs, send_sum, recv_sum, send_pair, recv_pair = refs.take(7)
        attended_rows, middle, unit_one, slope, active, grad_hidden = refs.take(6)
        me, other = group_me("core"), group_peer("core", 1)
        loads = [
            pltpu.make_async_copy(source, target, load_sems.at[at])
            for at, (source, target) in enumerate(
                ((output_hbm, output_w), (inner_hbm, inner_w), (outer_hbm, outer_w))
            )
        ]
        stores = [
            pltpu.make_async_copy(source, target, store_sems.at[at])
            for at, (source, target) in enumerate(
                ((grad_outer, grad_outer_hbm), (grad_inner, grad_inner_hbm), (grad_output, grad_output_hbm))
            )
        ]
        sums = [
            remote(partial.at[other], got.at[at], send_sum.at[at], recv_sum.at[at], "core", other)
            for at in range(3)
        ]
        gathers = [
            remote(pairs.at[at, me], pairs.at[at, me], send_pair.at[at], recv_pair.at[at], "core", other)
            for at in range(3)
        ]
        output_bias, first_gain, first_shift, outer_bias, second_gain, second_shift = (
            small_ref[at : at + 1, :] for at in range(6)
        )

        def pair_of(at):
            return pairs[at].reshape(PAIR, D)

        for load in loads:
            load.start()
        enter(["core"])
        attended_rows[...] = attended_ref[...].astype(F32).T.astype(BF).reshape(2, ROWS, D // 2)
        loads[0].wait()
        partial[other] = dot(attended_rows[other], output_w[...])
        sums[0].start()
        partial[me] = dot(attended_rows[me], output_w[...])
        sums[0].wait()
        hidden = rows_ref[...].astype(F32) + (partial[me] + got[0] + output_bias)
        normed, inverse_one = normalize(hidden)
        unit_one[...] = normed
        middle[...] = normed * first_gain + first_shift
        pairs[0, me] = middle[...].astype(BF)
        gathers[0].start()
        loads[1].wait()

        def inner_half(half):
            def one_tile(at, carry):
                here = pl.ds(pl.multiple_of(at * tile, tile), tile)
                value = dot(pairs[0, half], inner_w[:, here]) + bias_ref[:, here]
                part = 0.5 * (1.0 + lax.erf(value * (0.5**0.5)))
                active[half, :, here] = (value * part).astype(BF)
                density = jnp.exp(-0.5 * value * value) * ((2.0 * math.pi) ** -0.5)
                slope[half, :, here] = part + value * density
                return carry

            lax.fori_loop(0, units // tile, one_tile, 0)

        inner_half(me)
        gathers[0].wait()
        inner_half(other)
        loads[2].wait()
        partial[other] = dot(active[other], outer_w[...])
        sums[1].start()
        partial[me] = dot(active[me], outer_w[...])
        sums[1].wait()
        unit_two, inverse_two = normalize(middle[...] + (partial[me] + got[1] + outer_bias))
        result_ref[...] = (unit_two * second_gain + second_shift).astype(BF)
        upstream = upstream_ref[...].astype(F32)
        grad_mid = normalize_back(upstream, unit_two, inverse_two, second_gain)
        pairs[1, me] = grad_mid.astype(BF)
        gathers[1].start()
        middle[...] = grad_mid
        sums_ref[3:4, :] = sum_rows(grad_mid.astype(BF).astype(F32))
        sums_ref[4:5, :] = sum_rows(upstream * unit_two)
        sums_ref[5:6, :] = sum_rows(upstream)
        bias_sum_ref[...] = jnp.zeros_like(bias_sum_ref)

        def hidden_half(half):
            def one_tile(at, carry):
                here = pl.ds(pl.multiple_of(at * tile, tile), tile)
                value = dot(pairs[1, half], outer_w[here, :], ((1,), (1,)))
                value = (value * slope[half, :, here]).astype(BF)
                grad_hidden[half, :, here] = value
                bias_sum_ref[:, here] += sum_rows(value.astype(F32))
                return carry

            lax.fori_loop(0, units // tile, one_tile, 0)

        hidden_half(me)
        gathers[1].wait()
        hidden_half(other)
        partial[other] = dot(grad_hidden[other], inner_w[...], ((1,), (1,)))
        sums[2].start()
        partial[me] = dot(grad_hidden[me], inner_w[...], ((1,), (1,)))

        def outer_tile(at, carry):
            here = pl.ds(pl.multiple_of(at * tile, tile), tile)
            hidden = active[:, :, here].reshape(PAIR, tile)
            grad_outer[here, :] = dot(hidden, pair_of(1), ((0,), (0,))).astype(BF)
            return carry

        lax.fori_loop(0, units // tile, outer_tile, 0)
        stores[0].start()
        sums[2].wait()
        grad_middle = partial[me] + got[2] + middle[...]
        normed = unit_one[...]
        residual = normalize_back(grad_middle, normed, inverse_one, first_gain)
        pairs[2, me] = residual.astype(BF)
        gathers[2].start()
        residual_ref[...] = residual
        sums_ref[0:1, :] = sum_rows(residual.astype(BF).astype(F32))
        sums_ref[1:2, :] = sum_rows(grad_middle * normed)
        sums_ref[2:3, :] = sum_rows(grad_middle)
        sums_ref[6:8, :] = jnp.zeros((2, D), F32)

        def inner_tile(at, carry):
            here = pl.ds(pl.multiple_of(at * tile, tile), tile)
            hidden = grad_hidden[:, :, here].reshape(PAIR, tile)
            grad_inner[:, here] = dot(pair_of(0), hidden, ((0,), (0,))).astype(BF)
            return carry

        lax.fori_loop(0, units // tile, inner_tile, 0)
        stores[1].start()
        gathers[2].wait()
        grad_output[...] = dot(attended_ref[...], pair_of(2)).astype(BF)
        stores[2].start()
        turned_ref[...] = dot(output_w[...], pair_of(2), ((1,), (1,))).astype(BF)
        for store in stores:
            store.wait()

    grads = [(D // 2, D), (D, units), (units, D)]
    return pl.pallas_call(
        kernel,
        out_shape=[
            jax.ShapeDtypeStruct((ROWS, D), BF),
            jax.ShapeDtypeStruct((ROWS, D), F32),
            jax.ShapeDtypeStruct((D // 2, PAIR), BF),
            jax.ShapeDtypeStruct((8, D), F32),
            jax.ShapeDtypeStruct((1, units), F32),
        ]
        + [jax.ShapeDtypeStruct(shape, BF) for shape in grads],
        in_specs=[VMEM] * 5 + [ANY] * 3,
        out_specs=[VMEM] * 5 + [ANY] * 3,
        scratch_shapes=[pltpu.VMEM(shape, BF) for shape in grads]
        + [dma(3)]
        + [pltpu.VMEM(shape, BF) for shape in grads]
        + [
            dma(3),
            pltpu.VMEM((2, ROWS, D), F32),
            pltpu.VMEM((3, ROWS, D), F32),
            pltpu.VMEM((3, 2, ROWS, D), BF),
            dma(3),
            dma(3),
            dma(3),
            dma(3),
            pltpu.VMEM((2, ROWS, D // 2), BF),
            pltpu.VMEM((ROWS, D), F32),
            pltpu.VMEM((ROWS, D), F32),
            pltpu.VMEM((2, ROWS, units), F32),
            pltpu.VMEM((2, ROWS, units), BF),
            pltpu.VMEM((2, ROWS, units), BF),
        ],
        compiler_params=params(identifier, 56),
        name="feed_forward",
    )(rows, cotangent, attended, small, inner_bias, output_weight, inner_weight, outer_weight)


def per_device(
    tokens,
    cotangent,
    w_query,
    b_query,
    w_key,
    w_value,
    b_value,
    w_output,
    b_output,
    first_gain,
    first_shift,
    w_inner,
    b_inner,
    w_outer,
    b_outer,
    second_gain,
    second_shift,
):
    rows = tokens[0]

    small_part = jnp.concatenate(
        [
            jnp.stack(
                [b_query, b_value, b_output, first_gain, first_shift, b_outer, second_gain, second_shift]
            ),
            b_inner.reshape(4, 128),
            jnp.zeros((4, 128), BF),
        ]
    )
    (
        rows_turned,
        qkv_weight,
        rows_small,
        inner_bias,
        output_weight,
        inner_weight,
        outer_weight,
        qkv_got,
        summed,
        attended,
        stat,
    ) = forward(0, rows, w_query, w_key, w_value, small_part, w_output, w_inner, w_outer)
    (
        result,
        grad_residual,
        grad_attended,
        row_sums,
        grad_inner_bias,
        grad_output_weight,
        grad_inner_weight,
        grad_outer_weight,
    ) = feed_forward(
        1,
        rows,
        cotangent[0],
        attended.reshape(D // 2, PAIR),
        output_weight.reshape(D // 2, D),
        inner_weight.reshape(D, FF // 2),
        outer_weight.reshape(FF // 2, D),
        rows_small,
        inner_bias,
    )
    token_grad, *shares = backward(
        2,
        qkv_got,
        summed,
        stat,
        grad_attended.reshape(CHIPS, HD, PAIR),
        rows_turned,
        qkv_weight,
        grad_residual,
        row_sums,
        grad_inner_bias,
        grad_output_weight.reshape(SEQ, HD, D),
        grad_inner_weight.reshape(SEQ, 128, FF // 2),
        grad_outer_weight.reshape(SEQ, 256, D),
    )
    query, key, value, output, inner, outer, query_bias, value_bias, inner_bias, *whole = unpack(*shares)
    whole = [row.reshape(128) for row in whole]
    return (
        result[None],
        token_grad[None],
        query,
        query_bias.reshape(128),
        key,
        value,
        value_bias.reshape(128),
        output,
        whole[0],
        whole[1],
        whole[2],
        inner,
        inner_bias.reshape(512),
        outer,
        whole[3],
        whole[4],
        whole[5],
    )


def solution(mesh):
    row = P("seq", None)
    vector = P("seq")
    placed = P("seq", "ctx", None)
    return jax.shard_map(
        per_device,
        mesh=mesh,
        in_specs=(
            placed,
            placed,
            row,
            vector,
            row,
            row,
            vector,
            row,
            vector,
            vector,
            vector,
            row,
            vector,
            row,
            vector,
            vector,
            vector,
        ),
        out_specs=(
            placed,
            placed,
            row,
            vector,
            row,
            row,
            vector,
            row,
            vector,
            vector,
            vector,
            row,
            vector,
            row,
            vector,
            vector,
            vector,
        ),
        check_vma=False,
    )
```

profile of v0, /device:TPU:1, one launch (start us, length us, event | category | flops | bytes accessed | tf_op | source)
XLA Modules:
  0.0 287.6 jit_solution(17220620204445787260)
XLA Ops:
  0.7 1.5 concatenate.3.refs_4_
  2.2 0.0 copy-start
  2.2 1.0 copy-done
  3.2 1.2 copy-done.4
  4.4 0.9 copy-done.10
  5.3 0.9 copy-done.11
  6.3 0.9 copy-done.12
  7.2 0.9 copy-done.13
  8.2 101.0 %forward.1 = (bf16[1024,384]{1,0:T(8,128)(2,1)S(1)}, bf16[8,128,1536]{2,1,0:T(8,128)(2,1)}, f32[8,1024]{1,0:T(8,128)S(1)}, f32[1,2048]{1,0:T(1,128)S(1)}, bf16[8...) custom-call(bf16[192,1024]{1,0:T(8,128)(2,1)S(1)} %bitcast.31, ...), custom_call_target="tpu_custom_call" | custom-call | tf_op jit(solution)/shard_map/forward/pallas_call | solution.py:567
  109.2 0.0 copy-start.3
  109.2 1.0 copy-done.3
  110.1 0.9 copy-done.6
  111.0 0.9 copy-done.7
  111.9 0.7 copy-done.8
  112.6 0.6 copy-done.16
  113.3 0.6 copy-done.17
  113.9 0.6 copy-done.18
  114.5 33.9 %feed_forward.1 = (bf16[192,1024]{1,0:T(8,128)(2,1)}, f32[192,1024]{1,0:T(8,128)}, bf16[512,384]{1,0:T(8,128)(2,1)}, f32[8,1024]{1,0:T(8,128)}, f32[1,2048]{1,0:...) custom-call(bf16[192,1024]{1,0:T(8,128)(2,1)} %bitcast.30, ...), custom_call_target="tpu_custom_call" | custom-call | tf_op jit(solution)/shard_map/feed_forward/pallas_call | solution.py:1167
  148.4 0.0 copy-start.20
  148.4 128.2 %backward.1 = (f32[192,1024]{1,0:T(8,128)}, bf16[2,8,16,1536]{3,2,1,0:T(8,128)(2,1)}, bf16[2,4,16,1024]{3,2,1,0:T(8,128)(2,1)}, bf16[2,4,32,2048]{3,2,1,0:T(8,12...) custom-call(bf16[8,192,384]{2,1,0:T(8,128)(2,1)} %get-tuple-element.65.refs_0_, ...), custom_call_target="tpu_custom_call" | custom-call | tf_op jit(solution)/shard_map/backward/pallas_call | solution.py:867
  276.6 0.0 copy-start.1
  276.7 1.2 copy-done.1
  277.9 1.2 copy-done.2
  279.1 1.1 copy-done.5
  280.2 0.9 copy-done.9
  281.2 0.9 copy-done.14
  282.1 0.8 copy-done.15
  282.9 3.0 %unpack.1 = (f32[128,1024]{1,0:T(8,128)}, f32[128,1024]{1,0:T(8,128)}, f32[128,1024]{1,0:T(8,128)}, f32[128,1024]{1,0:T(8,128)}, f32[128,4096]{1,0:T(8,128)}, /*...) custom-call(bf16[2,8,16,1536]{3,2,1,0:T(8,128)(2,1)S(1)} %copy-done., ...), custom_call_target="tpu_custom_call" | custom-call | tf_op jit(solution)/shard_map/unpack/pallas_call | solution.py:994
  285.9 0.0 copy-done.20
  286.0 0.7 copy.36
  286.7 0.0 copy-done.19
  286.7 0.9 copy.37
  (18 shorter events, 0.0 us)
Async XLA Ops:
  2.2 1.0 copy-start
  3.2 1.2 copy-start.4
  4.4 0.9 copy-start.10
  5.3 0.9 copy-start.11
  6.3 0.9 copy-start.12
  7.2 0.9 copy-start.13
  109.2 1.0 copy-start.3
  110.1 0.9 copy-start.6
  111.0 0.9 copy-start.7
  111.9 0.7 copy-start.8
  112.6 0.6 copy-start.16
  113.3 0.6 copy-start.17
  113.9 0.6 copy-start.18
  148.4 137.5 %copy-start.20 = (bf16[192,1024]{1,0:T(8,128)(2,1)S(1)}, bf16[192,1024]{1,0:T(8,128)(2,1)}, u32[]{:S(2)}) copy-start(bf16[192,1024]{1,0:T(8,128)(2,1)} %get-tuple-element.64) | copy-start | bytes 1179652
  276.6 1.2 copy-start.1
  277.9 1.2 copy-start.2
  279.1 1.1 copy-start.5
  280.2 0.9 copy-start.9
  281.2 0.9 copy-start.14
  282.1 0.8 copy-start.15
  282.9 3.8 %copy-start.19 = (f32[192,1024]{1,0:T(8,128)S(1)}, f32[192,1024]{1,0:T(8,128)}, u32[]{:S(2)}) copy-start(f32[192,1024]{1,0:T(8,128)} %get-tuple-element.77) | copy-start | bytes 2359300
where the time goes:
time: 288 us
  Pallas kernels  266 us (92%)
  local copies, waits for them, and re-layouts  20.7 us (7%)
    pallas_call x1, Pallas kernels, backward(): pl.pallas_call(kernel, out_shape=[jax.ShapeDtypeStruct((ROWS, D), F32), j...  128 us
    pallas_call x1, Pallas kernels, forward(): pl.pallas_call(kernel, out_shape=[jax.ShapeDtypeStruct((D, PAIR), BF), ta...  101 us
    pallas_call x1, Pallas kernels, feed_forward(): pl.pallas_call(kernel, out_shape=[jax.ShapeDtypeStruct((ROWS, D), BF), ja...  33.9 us
    unnamed x44, local copies, waits for them, and re-layouts  19.2 us

commit v1 on v0

--- a/solution.py
+++ b/solution.py
@@ -502,7 +502,6 @@
         one_way.forward()
         split.forward_z()
         inner.start()
-        outer_two.start()
         other_way.forward()
         for one in (pair, small, qkv_own, one_way, other_way, split):
             one.wait()
@@ -516,9 +515,10 @@
             heads[chip, HD : 2 * HD, :] = part[HD : 2 * HD].astype(BF)
             heads[chip, 2 * HD :, :] = (part[2 * HD :] + shift[:, 1:2]).astype(BF)
         first.start()
+        inner.forward_z()
+        outer_two.start()
         output.start()
         outer_one.start()
-        inner.forward_z()
         output.forward()
         turned_out[...] = rows_out[...].reshape(PAIR, D).astype(F32).T.astype(BF)
         for owner in range(SEQ):
@@ -607,7 +607,7 @@
         + Own.scratch(output_part)
         + Own.scratch(inner_part)
         + Own.scratch(outer_part),
-        compiler_params=params(identifier, 48),
+        compiler_params=params(identifier, 62),
         name="forward",
     )(rows, w_query, w_key, w_value, small_part, w_output, w_inner, w_outer)
 
@@ -929,7 +929,7 @@
         + Spread.scratch("chip")
         + Spread.scratch("chip")
         + Spread.scratch("chip"),
-        compiler_params=params(identifier, 56),
+        compiler_params=params(identifier, 62),
         name="backward",
     )(
         qkv_got,
@@ -996,7 +996,7 @@
         out_shape=[jax.ShapeDtypeStruct(shape, F32) for shape in shapes],
         in_specs=[VMEM] * 6,
         out_specs=[VMEM] * 15,
-        compiler_params=pltpu.CompilerParams(vmem_limit_bytes=32 * 1024 * 1024),
+        compiler_params=pltpu.CompilerParams(vmem_limit_bytes=62 * 1024 * 1024),
         name="unpack",
     )(qkv, output, inner, outer, vectors, biases)
 
@@ -1195,7 +1195,7 @@
             pltpu.VMEM((2, ROWS, units), BF),
             pltpu.VMEM((2, ROWS, units), BF),
         ],
-        compiler_params=params(identifier, 56),
+        compiler_params=params(identifier, 62),
         name="feed_forward",
     )(rows, cotangent, attended, small, inner_bias, output_weight, inner_weight, outer_weight)
 

time: 288 us -> 268 us (0.931)
  local copies, waits for them, and re-layouts: 20.7 us -> 4.29 us
  Pallas kernels: 266 us -> 263 us
    unnamed x44 -> x6, local copies, waits for them, and re-layouts: 19.2 us -> 1.64 us
    pallas_call x1, Pallas kernels: 101 us -> 97.8 us  [forward(): pl.pallas_call(kernel, out_shape=[jax.ShapeDtypeStruct((D, PAIR), BF), ta...]
where the time goes in v1:
time: 268 us
  Pallas kernels  263 us (98%)
  local copies, waits for them, and re-layouts  4.29 us (2%)
    pallas_call x1, Pallas kernels, backward(): pl.pallas_call(kernel, out_shape=[jax.ShapeDtypeStruct((ROWS, D), F32), j...  126 us
    pallas_call x1, Pallas kernels, forward(): pl.pallas_call(kernel, out_shape=[jax.ShapeDtypeStruct((D, PAIR), BF), ta...  97.8 us
    pallas_call x1, Pallas kernels, feed_forward(): pl.pallas_call(kernel, out_shape=[jax.ShapeDtypeStruct((ROWS, D), BF), ja...  34 us

profile of v1, /device:TPU:1, one launch (start us, length us, event | category | flops | bytes accessed | tf_op | source)
XLA Modules:
  0.0 268.1 jit_solution(11521398192497618674)
XLA Ops:
  0.7 2.6 concatenate.3.refs_4_
  3.3 97.8 %forward.1 = (bf16[1024,384]{1,0:T(8,128)(2,1)}, bf16[8,128,1536]{2,1,0:T(8,128)(2,1)}, f32[8,1024]{1,0:T(8,128)}, f32[1,2048]{1,0:T(1,128)}, bf16[8,64,1024]{2,...) custom-call(bf16[192,1024]{1,0:T(8,128)(2,1)} %bitcast.34, ...), custom_call_target="tpu_custom_call" | custom-call | tf_op jit(solution)/shard_map/forward/pallas_call | solution.py:567
  101.1 34.0 %feed_forward.1 = (bf16[192,1024]{1,0:T(8,128)(2,1)}, f32[192,1024]{1,0:T(8,128)}, bf16[512,384]{1,0:T(8,128)(2,1)}, f32[8,1024]{1,0:T(8,128)}, f32[1,2048]{1,0:...) custom-call(bf16[192,1024]{1,0:T(8,128)(2,1)} %bitcast.35, ...), custom_call_target="tpu_custom_call" | custom-call | tf_op jit(solution)/shard_map/feed_forward/pallas_call | solution.py:1167
  135.1 0.0 copy-start.1
  135.1 126.4 %backward.1 = (f32[192,1024]{1,0:T(8,128)}, bf16[2,8,16,1536]{3,2,1,0:T(8,128)(2,1)}, bf16[2,4,16,1024]{3,2,1,0:T(8,128)(2,1)}, bf16[2,4,32,2048]{3,2,1,0:T(8,12...) custom-call(bf16[8,192,384]{2,1,0:T(8,128)(2,1)} %get-tuple-element.65.refs_0_, ...), custom_call_target="tpu_custom_call" | custom-call | tf_op jit(solution)/shard_map/backward/pallas_call | solution.py:867
  261.5 0.0 copy-start
  261.5 5.0 %unpack.1 = (f32[128,1024]{1,0:T(8,128)}, f32[128,1024]{1,0:T(8,128)}, f32[128,1024]{1,0:T(8,128)}, f32[128,1024]{1,0:T(8,128)}, f32[128,4096]{1,0:T(8,128)}, /*...) custom-call(bf16[2,8,16,1536]{3,2,1,0:T(8,128)(2,1)} %get-tuple-elem, ...), custom_call_target="tpu_custom_call" | custom-call | tf_op jit(solution)/shard_map/unpack/pallas_call | solution.py:994
  266.5 0.0 copy-done.1
  266.5 0.7 copy.36
  267.2 0.0 copy-done
  267.2 0.9 copy.37
  (1 shorter events, 0.0 us)
Async XLA Ops:
  135.1 131.4 %copy-start.1 = (bf16[192,1024]{1,0:T(8,128)(2,1)S(1)}, bf16[192,1024]{1,0:T(8,128)(2,1)}, u32[]{:S(2)}) copy-start(bf16[192,1024]{1,0:T(8,128)(2,1)} %get-tuple-element.64) | copy-start | bytes 1179652
  261.5 5.7 %copy-start = (f32[192,1024]{1,0:T(8,128)S(1)}, f32[192,1024]{1,0:T(8,128)}, u32[]{:S(2)}) copy-start(f32[192,1024]{1,0:T(8,128)} %get-tuple-element.77) | copy-start | bytes 2359300

commit v2 on v1

--- a/solution.py
+++ b/solution.py
@@ -840,11 +840,11 @@
         outer_mine[...] = outer_z.sum().astype(BF)
         outer_half.start()
         bias_all.start(bias_seq.sum())
+        inner_two.forward_z()
         upper = qkv_one.sum().reshape(CHIPS, 8, columns)
         lower = qkv_two.sum().reshape(CHIPS, 8, columns)
         qkv_sum[...] = jnp.concatenate([upper, lower], axis=1).astype(BF)
         qkv_chip.start()
-        inner_two.forward_z()
         output_all.start(output_half.sum())
         outer_all.start(outer_half.sum())
         inner_mine[:16] = inner_one.sum().astype(BF)

time: 268 us -> 268 us (level)
  no operation moved by 1% of the time
where the time goes in v2:
time: 268 us
  Pallas kernels  263 us (98%)
  local copies, waits for them, and re-layouts  4.29 us (2%)
    pallas_call x1, Pallas kernels, backward(): pl.pallas_call(kernel, out_shape=[jax.ShapeDtypeStruct((ROWS, D), F32), j...  126 us
    pallas_call x1, Pallas kernels, forward(): pl.pallas_call(kernel, out_shape=[jax.ShapeDtypeStruct((D, PAIR), BF), ta...  97.8 us
    pallas_call x1, Pallas kernels, feed_forward(): pl.pallas_call(kernel, out_shape=[jax.ShapeDtypeStruct((ROWS, D), BF), ja...  34 us

profile of v2, /device:TPU:1, one launch (start us, length us, event | category | flops | bytes accessed | tf_op | source)
XLA Modules:
  0.0 268.1 jit_solution(14670631932899411574)
XLA Ops:
  0.7 2.6 concatenate.3.refs_4_
  3.3 97.8 %forward.1 = (bf16[1024,384]{1,0:T(8,128)(2,1)}, bf16[8,128,1536]{2,1,0:T(8,128)(2,1)}, f32[8,1024]{1,0:T(8,128)}, f32[1,2048]{1,0:T(1,128)}, bf16[8,64,1024]{2,...) custom-call(bf16[192,1024]{1,0:T(8,128)(2,1)} %bitcast.34, ...), custom_call_target="tpu_custom_call" | custom-call | tf_op jit(solution)/shard_map/forward/pallas_call | solution.py:567
  101.1 34.0 %feed_forward.1 = (bf16[192,1024]{1,0:T(8,128)(2,1)}, f32[192,1024]{1,0:T(8,128)}, bf16[512,384]{1,0:T(8,128)(2,1)}, f32[8,1024]{1,0:T(8,128)}, f32[1,2048]{1,0:...) custom-call(bf16[192,1024]{1,0:T(8,128)(2,1)} %bitcast.35, ...), custom_call_target="tpu_custom_call" | custom-call | tf_op jit(solution)/shard_map/feed_forward/pallas_call | solution.py:1167
  135.1 0.0 copy-start.1
  135.1 126.4 %backward.1 = (f32[192,1024]{1,0:T(8,128)}, bf16[2,8,16,1536]{3,2,1,0:T(8,128)(2,1)}, bf16[2,4,16,1024]{3,2,1,0:T(8,128)(2,1)}, bf16[2,4,32,2048]{3,2,1,0:T(8,12...) custom-call(bf16[8,192,384]{2,1,0:T(8,128)(2,1)} %get-tuple-element.65.refs_0_, ...), custom_call_target="tpu_custom_call" | custom-call | tf_op jit(solution)/shard_map/backward/pallas_call | solution.py:867
  261.5 0.0 copy-start
  261.5 5.0 %unpack.1 = (f32[128,1024]{1,0:T(8,128)}, f32[128,1024]{1,0:T(8,128)}, f32[128,1024]{1,0:T(8,128)}, f32[128,1024]{1,0:T(8,128)}, f32[128,4096]{1,0:T(8,128)}, /*...) custom-call(bf16[2,8,16,1536]{3,2,1,0:T(8,128)(2,1)} %get-tuple-elem, ...), custom_call_target="tpu_custom_call" | custom-call | tf_op jit(solution)/shard_map/unpack/pallas_call | solution.py:994
  266.5 0.0 copy-done.1
  266.5 0.7 copy.36
  267.2 0.0 copy-done
  267.2 0.9 copy.37
  (1 shorter events, 0.0 us)
Async XLA Ops:
  135.1 131.4 %copy-start.1 = (bf16[192,1024]{1,0:T(8,128)(2,1)S(1)}, bf16[192,1024]{1,0:T(8,128)(2,1)}, u32[]{:S(2)}) copy-start(bf16[192,1024]{1,0:T(8,128)(2,1)} %get-tuple-element.64) | copy-start | bytes 1179652
  261.5 5.7 %copy-start = (f32[192,1024]{1,0:T(8,128)S(1)}, f32[192,1024]{1,0:T(8,128)}, u32[]{:S(2)}) copy-start(f32[192,1024]{1,0:T(8,128)} %get-tuple-element.77) | copy-start | bytes 2359300
